TPU v7x, 256 devices: a whole 4x4x8 slice. The times are simulated.
256 devices in a mesh: view: 16 (over z, core), span: 16 (over x, y).
Axes of the slice: x: 4, y: 4, z: 8, core: 2. Of those that a mesh axis runs over, the one named last changes fastest.
Arguments:
- tokens: bfloat16 [16, 4096, 1024], P('view', 'span'), may hold values from -6 to 6
- scan_order: int32 [16, 4096], P('view'), may hold values from 0 to 4095, as said below
- w_merge: bfloat16 [4096, 1024], replicated, may hold values from -0.09375 to 0.09375
- bias: bfloat16 [1024], replicated, may hold values from -4 to 4
- cotangent: bfloat16 [16, 1024, 1024], P('view', 'span'), may hold values from -6 to 6
Outputs:
- merged_out: bfloat16 [16, 1024, 1024], P('view', 'span')
- token_grad: bfloat16 [16, 4096, 1024], P('view', 'span')
- weight_grad: float32 [4096, 1024], P(('view', 'span'))
- bias_grad: float32 [1024], replicated
Inputs may be any that keep to these rules, and one draw needn't show every extreme that they name: `scan_order`: each row is a permutation of the raster indices of one view. Call tokens 256 * b to 256 * (b + 1) - 1 band b, and scan positions 256 * c to 256 * (c + 1) - 1 block c: every block holds at most 24 tokens of any band, and in every row each block holds exactly 24 tokens of some band.
All inputs are finite; a program needn't handle non-finite values.
Results may differ from a plain program's by a relative error of at most 0.001.
Values may be sent and summed in bfloat16 or wider, within the bound.
A program may use at most 128 MiB of HBM per device.

v0:
```python
import math
import jax
import jax.numpy as jnp
from jax import lax
from jax.sharding import PartitionSpec as P

COLS = 128


def body(tokens, scan_order, w_merge, bias, cotangent):
    spans = lax.axis_size("span")
    views = lax.axis_size("view")
    span_index = lax.axis_index("span")
    tok_dev = tokens.shape[1]
    width = tokens.shape[2]
    capacity = 3 * (tok_dev // spans) // 2
    rows_dev = tok_dev // COLS
    order_all = scan_order[0].reshape(spans, tok_dev)
    owners = order_all // tok_dev
    owner_hot = (owners[:, :, None] == jnp.arange(spans, dtype=jnp.int32)[None, None, :]).astype(
        jnp.int32
    )
    slot_rank = jnp.sum((jnp.cumsum(owner_hot, axis=1) - 1) * owner_hot, axis=2)
    dest_slots = owners * capacity + slot_rank
    my_slots = lax.dynamic_index_in_dim(dest_slots, span_index, 0, keepdims=False)
    outgoing = jnp.zeros((spans * capacity, width), jnp.bfloat16).at[my_slots].set(tokens[0])
    received = lax.all_to_all(
        outgoing.reshape(spans, capacity, width), "span", split_axis=0, concat_axis=0, tiled=True
    )
    arriving = owners == span_index
    source_slot = jnp.arange(spans, dtype=jnp.int32)[:, None] * capacity + slot_rank
    local_index = jnp.where(arriving, order_all - span_index * tok_dev, tok_dev)
    source_of = (
        jnp.zeros((tok_dev,), jnp.int32)
        .at[local_index.reshape(-1)]
        .set(source_slot.reshape(-1), mode="drop")
    )
    raster = received.reshape(spans * capacity, width)[source_of]
    merged = (
        raster.reshape(rows_dev // 2, 2, COLS // 2, 2, width)
        .transpose(0, 2, 1, 3, 4)
        .reshape(tok_dev // 4, 4 * width)
    )
    merged_out = (
        jnp.dot(merged, w_merge, preferred_element_type=jnp.float32) + bias.astype(jnp.float32)
    ).astype(jnp.bfloat16)
    grads = cotangent[0]
    grad_merged = lax.dot_general(
        grads, w_merge, (((1,), (1,)), ((), ())), preferred_element_type=jnp.float32
    ).astype(jnp.bfloat16)
    grad_raster = (
        grad_merged.reshape(rows_dev // 2, COLS // 2, 2, 2, width)
        .transpose(0, 2, 1, 3, 4)
        .reshape(tok_dev, width)
    )
    going_back = jnp.zeros((spans * capacity, width), jnp.bfloat16).at[source_of].set(grad_raster)
    returned = lax.all_to_all(
        going_back.reshape(spans, capacity, width), "span", split_axis=0, concat_axis=0, tiled=True
    )
    token_grad = returned.reshape(spans * capacity, width)[my_slots]
    weight_sum = lax.psum_scatter(
        lax.dot_general(
            merged, grads, (((0,), (0,)), ((), ())), preferred_element_type=jnp.float32
        ),
        ("view", "span"),
        scatter_dimension=0,
        tiled=True,
    )
    bias_total = lax.psum(jnp.sum(grads.astype(jnp.float32), axis=0), ("view", "span"))
    grad_scale = 1.0 / math.sqrt(views * spans * (tok_dev // 4))
    return (merged_out[None], token_grad[None], weight_sum * grad_scale, bias_total * grad_scale)


def solution(mesh):
    in_specs = (P("view", "span", None), P("view", None), P(), P(), P("view", "span", None))
    out_specs = (P("view", "span", None), P("view", "span", None), P(("view", "span"), None), P())
    return jax.shard_map(body, mesh=mesh, in_specs=in_specs, out_specs=out_specs, check_vma=False)
```

profile of v0, /device:TPU:0, one launch (start us, length us, event | category | flops | bytes accessed | tf_op | source)
XLA Modules:
  0.0 1363.6 jit_solution(8147675132378394235)
XLA Ops:
  7.2 0.0 copy-start
  7.2 0.0 copy-start.1
  7.2 0.8 and_select_fusion.1
  8.0 9.1 reduce-window.6
  17.1 0.1 slice.12
  17.3 0.3 copy.9
  17.5 0.1 fusion.14
  17.6 0.5 broadcast.237
  18.1 1.4 reduce.3
  19.6 0.1 fusion.8
  19.8 0.0 copy-done
  19.8 2.6 scatter_custom_fusion
  22.4 5.3 all-to-all-start
  27.7 0.0 reduce-scatter.2.cloned.1.call-start
  27.7 0.8 compare_select_fusion
  28.6 0.1 add_bitcast_fusion.1
  28.6 15.5 %scatter_custom_fusion.1 = s32[256]{0:T(256)S(1)} fusion(s32[4096]{0:T(1024)S(1)} %bitcast.73, s32[4096]{0:T(1024)S(1)} %bitcast.74, s32[]{:T(128)} %constant.19.clone.1), kind=kCustom, calls=%fused_computation.59 | custom fusion | bytes 1028 | tf_op jit(solution)/shard_map/scatter | solution.py:36
  44.2 0.0 all-to-all-done
  44.2 1.2 gather_fusion
  45.4 0.2 reshape.220
  45.6 0.4 copy.20
  45.9 0.4 reshape.221
  46.3 0.0 copy-done.1
  46.3 8.1 fusion.10
  54.4 0.0 reduce-scatter.2.cloned.1.call-update
  54.4 0.0 copy-start.2
  54.5 6.0 convolution_convert_fusion
  60.5 0.4 reshape.222
  60.9 0.4 copy.19
  61.3 0.2 reshape.262
  61.5 2.6 scatter_custom_fusion.2
  64.1 7.2 all-to-all-start.1
  71.3 0.0 copy-done.2
  71.3 83.0 %psum.7 = f32[1024]{0:T(1024)S(1)} all-reduce(f32[1024]{0:T(1024)S(1)} %convert_reduce_fusion), channel_id=1, replica_groups=mesh['view'=16,'span'=16] {'view','span'}, use_global_device_ids=true, to_apply=%region_8.9 | all-reduce | flops 1024 | bytes 8192 | tf_op jit(solution)/shard_map/psum | solution.py:69
  154.4 0.6 broadcast_multiply_fusion.1
  154.9 0.0 all-to-all-done.1
  155.0 2.0 gather_fusion.1
  156.9 5.6 fusion.1
  162.5 1192.8 %reduce-scatter.2.cloned.1.call-done = f32[16,1024]{1,0:T(8,128)} async-done(((f32[4096,1024]{1,0:T(8,128)}), f32[16,1024]{1,0:T(8,128)}) %reduce-scatter.2.cloned.1.call-update) | async-done | bytes 65552 | tf_op jit(solution)/shard_map/reduce_scatter | solution.py:61
  1355.3 1.5 broadcast_multiply_fusion
  (13 shorter events, 0.1 us)
Async XLA Ops:
  7.2 12.6 copy-start
  7.2 39.1 %copy-start.1 = (bf16[1,64,1024]{2,1,0:T(8,128)(2,1)S(1)}, bf16[1,64,1024]{2,1,0:T(8,128)(2,1)}, u32[]{:S(2)}) copy-start(bf16[1,64,1024]{2,1,0:T(8,128)(2,1)} %param.9) | copy-start | bytes 393220
  22.4 21.8 %all-to-all-start = ((bf16[16,24,1024]{2,1,0:T(8,128)(2,1)}), bf16[16,24,1024]{2,1,0:T(8,128)(2,1)S(1)}, u32[]{:S(2)}, u32[]{:S(2)}) async-start(bf16[16,24,1024]{2,1,0:T(8,128)(2,1)} %bitcast.6), calls=%async_computation | async-start | bytes 1572864 | tf_op jit(solution)/shard_map/all_to_all | solution.py:27
  27.7 1327.7 %reduce-scatter.2.cloned.1.call-start = ((), (), s32[]{:S(2)}) async-start(), calls=%async_computation.3 | async-start | bytes 16842752 | tf_op jit(solution)/shard_map/reduce_scatter | solution.py:61
  54.4 16.8 %copy-start.2 = (bf16[1024]{0:T(1024)(128)(2,1)S(1)}, bf16[1024]{0:T(1024)(128)(2,1)}, u32[]{:S(2)}) copy-start(bf16[1024]{0:T(1024)(128)(2,1)} %param.8) | copy-start | bytes 6148
  64.1 90.9 %all-to-all-start.1 = ((bf16[16,24,1024]{2,1,0:T(8,128)(2,1)}), bf16[16,24,1024]{2,1,0:T(8,128)(2,1)S(1)}, u32[]{:S(2)}, u32[]{:S(2)}) async-start(bf16[16,24,1024]{2,1,0:T(8,128)(2,1)} %bitcast.14), calls=%async_computation.1 | async-start | bytes 1572864 | tf_op jit(solution)/shard_map/all_to_all | solution.py:57
Sparse Core Ops, SparseCore 0:
  54.6 1300.7 reduce-scatter.1
where the time goes:
time: 1360 us
  waiting for transfers between devices  1190 us (88%)
  blocking collectives  83 us (6%)
  local copies, waits for them, and re-layouts  26.7 us (2%)
  matrix products  19.8 us (1%)
  other arithmetic  14.6 us (1%)
  between operations  14.3 us (1%)
    reduce_scatter x1, waiting for transfers between devices, body(): lax.psum_scatter(lax.dot_general(merged, grads, (((0,), (0,)), ((), ())),...  1190 us
    psum x1, blocking collectives, body(): lax.psum(jnp.sum(grads.astype(jnp.float32), axis=0), ('view', 'span'))  83 us
  transfers between devices with their start and end apart: 3, of which 1 were waited for; matrix products, arithmetic and copies ran while one was open for 3% of the time, Pallas kernels for 0%

commit v1 on v0

--- a/solution.py
+++ b/solution.py
@@ -66,7 +66,9 @@
         scatter_dimension=0,
         tiled=True,
     )
-    bias_total = lax.psum(jnp.sum(grads.astype(jnp.float32), axis=0), ("view", "span"))
+    bias_total = jnp.sum(
+        lax.all_gather(jnp.sum(grads.astype(jnp.float32), axis=0), ("view", "span")), axis=0
+    )
     grad_scale = 1.0 / math.sqrt(views * spans * (tok_dev // 4))
     return (merged_out[None], token_grad[None], weight_sum * grad_scale, bias_total * grad_scale)
 

time: 1360 us -> 1450 us (1.066)
  waiting for transfers between devices: 1190 us -> 1360 us
  blocking collectives: 83 us -> 0 us
    reduce_scatter x1, waiting for transfers between devices: 1190 us -> 1300 us  [body(): lax.psum_scatter(lax.dot_general(merged, grads, (((0,), (0,)), ((), ())),...]
    psum x1 -> x0, blocking collectives: 83 us -> none  [body(): lax.psum(jnp.sum(grads.astype(jnp.float32), axis=0), ('view', 'span'))]
    all_gather x0 -> x1, waiting for transfers between devices: none -> 46 us  [body(): lax.all_gather(jnp.sum(grads.astype(jnp.float32), axis=0), ('view', 'span'))]
  transfers between devices with their start and end apart: 3 -> 4, of which waited for: 1 -> 3; matrix products, arithmetic and copies ran while one was open for 3% -> 3% of each run, Pallas kernels for 0% -> 0%
where the time goes in v1:
time: 1450 us
  waiting for transfers between devices  1360 us (94%)
  local copies, waits for them, and re-layouts  28.3 us (2%)
  matrix products  19.7 us (1%)
  other arithmetic  16.2 us (1%)
    reduce_scatter x1, waiting for transfers between devices, body(): lax.psum_scatter(lax.dot_general(merged, grads, (((0,), (0,)), ((), ())),...  1300 us
    all_gather x1, waiting for transfers between devices, body(): lax.all_gather(jnp.sum(grads.astype(jnp.float32), axis=0), ('view', 'span'))  46 us
  transfers between devices with their start and end apart: 4, of which 3 were waited for; matrix products, arithmetic and copies ran while one was open for 3% of the time, Pallas kernels for 0%

profile of v1, /device:TPU:0, one launch (start us, length us, event | category | flops | bytes accessed | tf_op | source)
XLA Modules:
  0.0 1447.9 jit_solution(1575076148358850291)
XLA Ops:
  7.2 0.0 copy-start
  7.2 0.0 copy-start.1
  7.2 0.8 and_select_fusion.1
  8.0 9.1 reduce-window.6
  17.1 0.1 slice.12
  17.3 0.3 copy.19
  17.5 0.1 fusion.14
  17.6 0.5 broadcast.237
  18.1 1.4 reduce.3
  19.6 0.1 fusion.8
  19.8 0.0 copy-done
  19.8 2.6 scatter_custom_fusion
  22.4 5.3 all-to-all-start
  27.7 0.0 all-gather.3.cloned.1.call-start
  27.7 1.5 convert_reduce_fusion
  29.2 0.0 all-gather.3.cloned.1.call-update
  29.3 0.0 reduce-scatter.2.cloned.1.call-start
  29.3 0.8 compare_select_fusion
  30.2 0.1 add_bitcast_fusion.1
  30.2 15.7 %scatter_custom_fusion.1 = s32[256]{0:T(256)S(1)} fusion(s32[4096]{0:T(1024)S(1)} %bitcast.73, s32[4096]{0:T(1024)S(1)} %bitcast.74, s32[]{:T(128)} %constant.19.clone.1), kind=kCustom, calls=%fused_computation.59 | custom fusion | bytes 1028 | tf_op jit(solution)/shard_map/scatter | solution.py:36
  46.0 0.0 all-to-all-done
  46.0 1.2 gather_fusion
  47.1 0.2 reshape.220
  47.3 0.4 copy.30
  47.7 0.4 reshape.221
  48.1 0.0 copy-done.1
  48.1 8.1 fusion.10
  56.2 0.0 reduce-scatter.2.cloned.1.call-update
  56.2 0.0 copy-start.2
  56.2 6.0 convolution_convert_fusion
  62.3 0.4 reshape.222
  62.7 0.4 copy.29
  63.0 0.2 reshape.262
  63.2 2.6 scatter_custom_fusion.2
  65.9 7.2 all-to-all-start.1
  73.1 0.0 copy-done.2
  73.2 13.7 all-to-all-done.1
  86.9 2.0 gather_fusion.1
  88.9 5.6 fusion.1
  94.5 46.0 %all-gather.3.cloned.1.call-done = f32[262144]{0:T(1024)} async-done(((f32[1024]{0:T(1024)}), f32[262144]{0:T(1024)}) %all-gather.3.cloned.1.call-update) | async-done | bytes 1048592 | tf_op jit(solution)/shard_map/all_gather | solution.py:70
  140.4 1.4 reshape.266
  141.8 0.1 reduce_sum.29
  141.9 0.6 broadcast_multiply_fusion.1
  142.5 1297.1 %reduce-scatter.2.cloned.1.call-done = f32[16,1024]{1,0:T(8,128)} async-done(((f32[4096,1024]{1,0:T(8,128)}), f32[16,1024]{1,0:T(8,128)}) %reduce-scatter.2.cloned.1.call-update) | async-done | bytes 65552 | tf_op jit(solution)/shard_map/reduce_scatter | solution.py:61
  1439.6 1.5 broadcast_multiply_fusion
  (12 shorter events, 0.1 us)
Async XLA Ops:
  7.2 12.6 copy-start
  7.2 40.9 %copy-start.1 = (bf16[1,64,1024]{2,1,0:T(8,128)(2,1)S(1)}, bf16[1,64,1024]{2,1,0:T(8,128)(2,1)}, u32[]{:S(2)}) copy-start(bf16[1,64,1024]{2,1,0:T(8,128)(2,1)} %param.9) | copy-start | bytes 393220
  22.4 23.6 %all-to-all-start = ((bf16[16,24,1024]{2,1,0:T(8,128)(2,1)}), bf16[16,24,1024]{2,1,0:T(8,128)(2,1)S(1)}, u32[]{:S(2)}, u32[]{:S(2)}) async-start(bf16[16,24,1024]{2,1,0:T(8,128)(2,1)} %bitcast.6), calls=%async_computation | async-start | bytes 1572864 | tf_op jit(solution)/shard_map/all_to_all | solution.py:27
  27.7 112.8 %all-gather.3.cloned.1.call-start = ((), (), s32[]{:S(2)}) async-start(), calls=%async_computation.4 | async-start | bytes 1052672 | tf_op jit(solution)/shard_map/all_gather | solution.py:70
  29.3 1410.3 %reduce-scatter.2.cloned.1.call-start = ((), (), s32[]{:S(2)}) async-start(), calls=%async_computation.3 | async-start | bytes 16842752 | tf_op jit(solution)/shard_map/reduce_scatter | solution.py:61
  56.2 16.9 %copy-start.2 = (bf16[1024]{0:T(1024)(128)(2,1)S(1)}, bf16[1024]{0:T(1024)(128)(2,1)}, u32[]{:S(2)}) copy-start(bf16[1024]{0:T(1024)(128)(2,1)} %param.8) | copy-start | bytes 6148
  65.9 21.0 %all-to-all-start.1 = ((bf16[16,24,1024]{2,1,0:T(8,128)(2,1)}), bf16[16,24,1024]{2,1,0:T(8,128)(2,1)S(1)}, u32[]{:S(2)}, u32[]{:S(2)}) async-start(bf16[16,24,1024]{2,1,0:T(8,128)(2,1)} %bitcast.14), calls=%async_computation.1 | async-start | bytes 1572864 | tf_op jit(solution)/shard_map/all_to_all | solution.py:57
Sparse Core Ops, SparseCore 0:
  32.8 107.5 all-gather.2
  142.9 1296.5 reduce-scatter.1
